TPU v7x, 32 devices: a whole 2x2x4 slice. The times are simulated.
32 devices in a mesh: member: 8 (over z, core), state: 4 (over y, x).
Axes of the slice: x: 2, y: 2, z: 4, core: 2. Of those that a mesh axis runs over, the one named last changes fastest.
Arguments:
- prior_analyses: float32 [64, 256, 1024], P('member', 'state'), may hold values from -6 to 6
- smoothing_number: float32 [256, 1024], P('state'), may hold values from 0.08 to 0.24
- observations: float32 [3072], replicated, may hold values from -6 to 6
- obs_variance: float32 [3072], replicated, may hold values from 0.25 to 2
- obs_row: int32 [3072], replicated, may hold values from 0 to 255
- obs_col: int32 [3072], replicated, may hold values from 0 to 1023
- obs_radius: int32 [3072], replicated, may hold values from 32 to 127
- block_order: int32 [3072], replicated, may hold values from 0 to 3071, each once
Outputs:
- analysis: float32 [64, 256, 1024], P('member', 'state')
Inputs may be any that keep to these rules, and one draw needn't show every extreme that they name: `block_order`: every observation index appears exactly once.
All inputs are finite; a program needn't handle non-finite values.
Results may differ from a plain program's by a relative error of at most 0.0035.
Values sent between devices are 32-bit elements; how exact they have to be, the bound alone decides.
A program may use at most 64 MiB of HBM per device.

v0:
```python
import jax
import jax.numpy as jnp
from jax import lax
from jax.sharding import PartitionSpec as P

BLK = 512
NBLK = 6
spread_eps = 1e-06


def extended(shard, sides, width):
    for axis, dim in sides:
        peers, length = (lax.axis_size(axis), shard.shape[dim])
        up = [(i, (i + 1) % peers) for i in range(peers - 1)]
        down = [(j, i) for i, j in up]
        last = lax.slice_in_dim(shard, length - width, length, axis=dim)
        leading = lax.slice_in_dim(shard, 0, width, axis=dim)
        before = lax.ppermute(last, axis, up)
        after = lax.ppermute(leading, axis, down)
        shard = jnp.concatenate([before, shard, after], axis=dim)
    return shard


def advance(padded, spreading_coefficients):
    center = padded[:, 1:-1, :]
    vertical = padded[:, 2:, :] + padded[:, :-2, :]
    sideways = jnp.pad(center[:, :, 1:], ((0, 0), (0, 0), (0, 1))) + jnp.pad(
        center[:, :, :-1], ((0, 0), (0, 0), (1, 0))
    )
    return center + spreading_coefficients * (vertical + sideways - 4.0 * center)


def predicted_level(realization_vectors, spreading_coefficients):
    current = realization_vectors
    for step_index in range(2):
        padded = extended(current, (("state", 1),), 1)
        current = advance(padded, spreading_coefficients)
    return current


def increments(prior_values, value_array, variances):
    realization_vectors = prior_values.shape[0]
    prior_mean = jnp.mean(prior_values, axis=0)
    anomaly = prior_values - prior_mean
    spread = jnp.sum(anomaly * anomaly, axis=0) / (realization_vectors - 1) + spread_eps
    post_var = spread * variances / (spread + variances)
    posterior_average = post_var * (prior_mean / spread + value_array / variances)
    shrink = jnp.sqrt(variances / (variances + spread)) - 1.0
    increment = (posterior_average - prior_mean + shrink * anomaly).astype(jnp.bfloat16)
    return (anomaly.astype(jnp.bfloat16), increment, 1.0 / spread)


def taper_weight(cell_row, cell_col, obs_rows, obs_cols, radius):
    row_gap = cell_row[None, :] - obs_rows[:, None]
    col_gap = cell_col[None, :] - obs_cols[:, None]
    distance = (row_gap * row_gap + col_gap * col_gap).astype(jnp.float32)
    reach = radius.astype(jnp.float32)
    closeness = jnp.maximum(1.0 - distance / (reach * reach)[:, None], 0.0)
    return closeness * closeness


def linear_gain_fit(
    target, target_rows, target_cols, anomaly, increment, inverse, obs_rows, obs_cols, radius
):
    realization_vectors = target.shape[0]
    cell_mean = jnp.mean(target, axis=0)
    cell_anomaly = (target - cell_mean).astype(jnp.bfloat16)
    sub_size = min(anomaly.shape[1], 128)
    accumulated = jnp.zeros(target.shape, jnp.float32)
    for part_index in range(anomaly.shape[1] // sub_size):
        lower_end = part_index * sub_size
        upper_end = lower_end + sub_size
        covariance = lax.dot_general(
            anomaly[:, lower_end:upper_end],
            cell_anomaly,
            (((0,), (0,)), ((), ())),
            preferred_element_type=jnp.float32,
        ) / (realization_vectors - 1)
        weight = taper_weight(
            target_rows,
            target_cols,
            obs_rows[lower_end:upper_end],
            obs_cols[lower_end:upper_end],
            radius[lower_end:upper_end],
        )
        gain_tile = (weight * covariance * inverse[lower_end:upper_end, None]).astype(jnp.bfloat16)
        accumulated = accumulated + jnp.dot(
            increment[:, lower_end:upper_end], gain_tile, preferred_element_type=jnp.float32
        )
    return accumulated


def pick_values(cell_values, rows_wanted, cols_wanted, first_row, tile_rows, tile_cols):
    local_row = rows_wanted - first_row
    inside = (
        (local_row >= 0) & (local_row < tile_rows) & (cols_wanted >= 0) & (cols_wanted < tile_cols)
    )
    local_index = jnp.where(inside, local_row * tile_cols + cols_wanted, 0)
    return jnp.where(inside[None, :], jnp.take(cell_values, local_index, axis=1), 0.0)


def on_device(
    prior_analyses,
    smoothing_number,
    observations,
    obs_variance,
    obs_row,
    obs_col,
    obs_radius,
    block_order,
):
    realization_vectors = predicted_level(prior_analyses, smoothing_number)
    row_count = realization_vectors.shape[1]
    col_count = realization_vectors.shape[2]
    member_count = lax.axis_size("member")
    base_row = lax.axis_index("state") * row_count
    tile_data = lax.all_to_all(
        realization_vectors, "member", split_axis=1, concat_axis=0, tiled=True
    )
    tile_rows = row_count // member_count
    first_row = base_row + lax.axis_index("member") * tile_rows
    grid_point_total = tile_rows * col_count
    cell_values = tile_data.reshape(tile_data.shape[0], grid_point_total)
    position = jnp.arange(grid_point_total, dtype=jnp.int32)
    cell_row = first_row + position // col_count
    cell_col = position % col_count
    for block_index in range(NBLK):
        chosen = block_order[block_index * BLK : (block_index + 1) * BLK]
        block_rows = jnp.take(obs_row, chosen)
        block_cols = jnp.take(obs_col, chosen)
        block_radius = jnp.take(obs_radius, chosen)
        local_values = pick_values(
            cell_values, block_rows, block_cols, first_row, tile_rows, col_count
        )
        prior_values = lax.psum(local_values, ("member", "state"))
        anomaly, increment, inverse = increments(
            prior_values, jnp.take(observations, chosen), jnp.take(obs_variance, chosen)
        )
        cell_values = cell_values + linear_gain_fit(
            cell_values,
            cell_row,
            cell_col,
            anomaly,
            increment,
            inverse,
            block_rows,
            block_cols,
            block_radius,
        )
    result = cell_values.reshape(tile_data.shape)
    return lax.all_to_all(result, "member", split_axis=0, concat_axis=1, tiled=True)


def solution(mesh):
    in_specs = (P("member", "state", None), P("state", None), P(), P(), P(), P(), P(), P())
    out_specs = P("member", "state", None)
    return jax.shard_map(
        on_device, mesh=mesh, in_specs=in_specs, out_specs=out_specs, check_vma=False
    )
```

profile of v0, /device:TPU:0, one launch (start us, length us, event | category | flops | bytes accessed | tf_op | source)
XLA Modules:
  0.0 1187.5 jit_solution(11396176168441743626)
XLA Ops:
  9.4 4.8 collective-permute-start.1
  18.4 3.3 gather_fusion.11
  107.2 4.3 gather_fusion.34
  111.4 4.2 gather_fusion.33
  115.7 3.4 fusion.87
  119.0 4.5 collective-permute-start.3
  126.2 3.6 collective-permute-done.2
  132.1 4.9 all-to-all-start
  140.1 45.9 %all-to-all-done = f32[8,64,1024]{2,0,1:T(8,128)S(1)} async-done(((f32[8,64,1024]{2,0,1:T(8,128)}), f32[8,64,1024]{2,0,1:T(8,128)S(1)}, u32[]{:S(2)}, u32[]{:S(2)}) %all-to-all-start) | async-done | bytes 2097184 | tf_op jit(solution)/shard_map/all_to_all | solution.py:117
  188.8 3.2 gather_fusion.2
  193.2 124.2 %all-reduce.11.cloned.1.call-done = f32[64,512]{0,1:T(8,128)} async-done(((f32[64,512]{0,1:T(8,128)}), f32[64,512]{0,1:T(8,128)}) %all-reduce.11.cloned.1.call-update) | async-done | bytes 131088 | tf_op jit(solution)/shard_map/psum | solution.py:135
  321.0 3.9 fusion.93
  324.9 5.6 convolution_add_fusion.17
  330.4 5.6 convolution_add_fusion.16
  336.0 5.7 fusion.292
  341.7 4.0 copy.34
  345.7 3.2 gather_fusion.8
  350.1 123.9 %all-reduce.13.cloned.1.call-done = f32[64,512]{0,1:T(8,128)} async-done(((f32[64,512]{0,1:T(8,128)}), f32[64,512]{0,1:T(8,128)}) %all-reduce.13.cloned.1.call-update) | async-done | bytes 131088 | tf_op jit(solution)/shard_map/psum | solution.py:135
  477.5 3.9 fusion.92
  481.4 5.6 convolution_add_fusion.14
  487.0 5.6 convolution_add_fusion.13
  492.6 5.7 fusion.295
  498.3 4.0 copy.35
  502.2 3.2 gather_fusion.14
  506.7 123.9 %all-reduce.15.cloned.1.call-done = f32[64,512]{0,1:T(8,128)} async-done(((f32[64,512]{0,1:T(8,128)}), f32[64,512]{0,1:T(8,128)}) %all-reduce.15.cloned.1.call-update) | async-done | bytes 131088 | tf_op jit(solution)/shard_map/psum | solution.py:135
  634.1 3.9 fusion.91
  638.0 5.6 convolution_add_fusion.11
  643.6 5.6 convolution_add_fusion.10
  649.2 5.6 fusion.298
  662.2 123.7 %all-reduce.17.cloned.1.call-done = f32[64,512]{0,1:T(8,128)} async-done(((f32[64,512]{0,1:T(8,128)}), f32[64,512]{0,1:T(8,128)}) %all-reduce.17.cloned.1.call-update) | async-done | bytes 131088 | tf_op jit(solution)/shard_map/psum | solution.py:135
  789.4 3.9 fusion.90
  793.3 5.6 convolution_add_fusion.8
  798.9 5.6 convolution_add_fusion.7
  804.4 5.7 fusion.301
  810.2 4.0 copy.37
  818.5 123.9 %all-reduce.19.cloned.1.call-done = f32[64,512]{0,1:T(8,128)} async-done(((f32[64,512]{0,1:T(8,128)}), f32[64,512]{0,1:T(8,128)}) %all-reduce.19.cloned.1.call-update) | async-done | bytes 131088 | tf_op jit(solution)/shard_map/psum | solution.py:135
  946.0 3.9 fusion.89
  949.9 5.6 convolution_add_fusion.5
  955.5 5.6 convolution_add_fusion.4
  961.0 5.7 fusion.304
  966.8 3.9 copy.38
  970.8 3.4 gather_fusion.32
  975.2 124.1 %all-reduce.21.cloned.1.call-done = f32[64,512]{0,1:T(8,128)} async-done(((f32[64,512]{0,1:T(8,128)}), f32[64,512]{0,1:T(8,128)}) %all-reduce.21.cloned.1.call-update) | async-done | bytes 131088 | tf_op jit(solution)/shard_map/psum | solution.py:135
  1103.0 3.9 fusion.88
  1106.9 5.6 convolution_add_fusion.2
  1112.5 5.6 convolution_add_fusion.1
  1118.1 5.7 fusion.72
  1126.6 52.4 %all_to_all.33 = f32[64,8,1024]{2,1,0:T(8,128)S(1)} all-to-all(f32[64,8,1024]{2,1,0:T(8,128)S(1)} %bitcast.36), channel_id=1, replica_groups=mesh['member'=8,'state'=4] {'member'}, dimensions={0} | all-to-all | bytes 4194304 | tf_op jit(solution)/shard_map/all_to_all | solution.py:151
  (205 shorter events, 144.2 us)
Async XLA Ops:
  6.5 11.9 copy-start
  9.4 106.3 %collective-permute-start.1 = (f32[8,1,1024]{2,0,1:T(8,128)S(1)}, f32[8,1,1024]{2,0,1:T(8,128)S(1)}, u32[]{:S(2)}, u32[]{:S(2)}) collective-permute-start(f32[8,1,1024]{2,0,1:T(8,128)S(1)} %get-tuple-element.57), channel_id=1, source_target_pairs={{0,1},{1,2},{2,3},{4,5},{5,6},{6,7},{8,9},{9,10},{10,11},{12,13},{... | collective-permute-start | bytes 98312 | tf_op jit(solution)/shard_map/ppermute | solution.py:18
  14.2 4.1 copy-start.11
  14.2 101.4 %collective-permute-start = (f32[8,1,1024]{2,0,1:T(8,128)S(1)}, f32[8,1,1024]{2,0,1:T(8,128)S(1)}, u32[]{:S(2)}, u32[]{:S(2)}) collective-permute-start(f32[8,1,1024]{2,0,1:T(8,128)S(1)} %get-tuple-element.56), channel_id=1, source_target_pairs={{1,0},{2,1},{3,2},{5,4},{6,5},{7,6},{9,8},{10,9},{11,10},{13,12},{... | collective-permute-start | bytes 98312 | tf_op jit(solution)/shard_map/ppermute | solution.py:19
  18.3 6.5 copy-start.2
  18.4 12.8 %copy-start.3 = (s32[3072]{0:T(1024)S(1)}, s32[3072]{0:T(1024)}, u32[]{:S(2)}) copy-start(s32[3072]{0:T(1024)} %param.19) | copy-start | bytes 36868
  50.1 12.9 %copy-start.4 = (f32[3072]{0:T(1024)S(1)}, f32[3072]{0:T(1024)}, u32[]{:S(2)}) copy-start(f32[3072]{0:T(1024)} %param.16) | copy-start | bytes 36868
  56.5 12.9 %copy-start.5 = (f32[3072]{0:T(1024)S(1)}, f32[3072]{0:T(1024)}, u32[]{:S(2)}) copy-start(f32[3072]{0:T(1024)} %param.17) | copy-start | bytes 36868
  62.8 74.2 %copy-start.15 = (pred[512]{0:T(512)(128)(4,1)}, pred[512]{0:T(512)(128)(4,1)S(1)}, u32[]{:S(2)}) copy-start(pred[512]{0:T(512)(128)(4,1)S(1)} %get-tuple-element.8) | copy-start | bytes 1540
  100.8 14.8 %copy-start.10 = (f32[64,1024]{1,0:T(8,128)S(1)}, f32[64,1024]{1,0:T(8,128)}, u32[]{:S(2)}) copy-start(f32[64,1024]{1,0:T(8,128)} %param.15) | copy-start | bytes 786436
  119.0 7.1 collective-permute-start.3
  123.6 6.2 collective-permute-start.2
  132.1 53.9 %all-to-all-start = ((f32[8,64,1024]{2,0,1:T(8,128)}), f32[8,64,1024]{2,0,1:T(8,128)S(1)}, u32[]{:S(2)}, u32[]{:S(2)}) async-start(f32[8,64,1024]{2,0,1:T(8,128)} %fusion.82), calls=%async_computation | async-start | bytes 4194304 | tf_op jit(solution)/shard_map/all_to_all | solution.py:117
  137.0 180.5 %all-reduce.11.cloned.1.call-start = ((), (), s32[]{:S(2)}) async-start(), calls=%async_computation.2 | async-start | bytes 524288 | tf_op jit(solution)/shard_map/psum | solution.py:135
  192.9 281.1 %all-reduce.13.cloned.1.call-start = ((), (), s32[]{:S(2)}) async-start(), calls=%async_computation.3 | async-start | bytes 524288 | tf_op jit(solution)/shard_map/psum | solution.py:135
  341.7 135.8 %copy-start.6 = (f32[64,8192]{1,0:T(8,128)S(1)}, f32[64,8192]{1,0:T(8,128)}, u32[]{:S(2)}) copy-start(f32[64,8192]{1,0:T(8,128)} %get-tuple-element.201) | copy-start | bytes 6291460
  349.8 280.7 %all-reduce.15.cloned.1.call-start = ((), (), s32[]{:S(2)}) async-start(), calls=%async_computation.4 | async-start | bytes 524288 | tf_op jit(solution)/shard_map/psum | solution.py:135
  498.3 135.8 %copy-start.7 = (f32[64,8192]{1,0:T(8,128)S(1)}, f32[64,8192]{1,0:T(8,128)}, u32[]{:S(2)}) copy-start(f32[64,8192]{1,0:T(8,128)} %get-tuple-element.203) | copy-start | bytes 6291460
  506.4 279.5 %all-reduce.17.cloned.1.call-start = ((), (), s32[]{:S(2)}) async-start(), calls=%async_computation.5 | async-start | bytes 524288 | tf_op jit(solution)/shard_map/psum | solution.py:135
  661.7 280.7 %all-reduce.19.cloned.1.call-start = ((), (), s32[]{:S(2)}) async-start(), calls=%async_computation.6 | async-start | bytes 524288 | tf_op jit(solution)/shard_map/psum | solution.py:135
  810.2 135.8 %copy-start.8 = (f32[64,8192]{1,0:T(8,128)S(1)}, f32[64,8192]{1,0:T(8,128)}, u32[]{:S(2)}) copy-start(f32[64,8192]{1,0:T(8,128)} %get-tuple-element.207) | copy-start | bytes 6291460
  818.3 281.0 %all-reduce.21.cloned.1.call-start = ((), (), s32[]{:S(2)}) async-start(), calls=%async_computation.7 | async-start | bytes 524288 | tf_op jit(solution)/shard_map/psum | solution.py:135
  966.8 4.0 copy-start.12
  966.8 7.5 copy-start.17
  966.8 7.5 copy-start.18
  966.8 134.8 %copy-start.13 = (f32[512]{0:T(512)S(1)}, f32[512]{0:T(512)}, u32[]{:S(2)}) copy-start(f32[512]{0:T(512)} %gather_fusion.34) | copy-start | bytes 6148
  966.8 134.8 %copy-start.14 = (f32[512]{0:T(512)S(1)}, f32[512]{0:T(512)}, u32[]{:S(2)}) copy-start(f32[512]{0:T(512)} %gather_fusion.33) | copy-start | bytes 6148
  966.8 134.8 %copy-start.16 = (pred[512]{0:T(512)(128)(4,1)S(1)}, pred[512]{0:T(512)(128)(4,1)}, u32[]{:S(2)}) copy-start(pred[512]{0:T(512)(128)(4,1)} %copy-done.15) | copy-start | bytes 1540
  966.8 136.1 %copy-start.9 = (f32[64,8192]{1,0:T(8,128)S(1)}, f32[64,8192]{1,0:T(8,128)}, u32[]{:S(2)}) copy-start(f32[64,8192]{1,0:T(8,128)} %get-tuple-element.209) | copy-start | bytes 6291460
  966.8 136.1 %copy-start.25 = (s32[128]{0:T(128)S(1)}, s32[128]{0:T(128)}, u32[]{:S(2)}) copy-start(s32[128]{0:T(128)} %get-tuple-element.101) | copy-start | bytes 1540
  966.8 136.1 %copy-start.26 = (s32[128]{0:T(128)S(1)}, s32[128]{0:T(128)}, u32[]{:S(2)}) copy-start(s32[128]{0:T(128)} %get-tuple-element.237) | copy-start | bytes 1540
  966.8 136.1 %copy-start.30 = (f32[128]{0:T(128)S(1)}, f32[128]{0:T(128)}, u32[]{:S(2)}) copy-start(f32[128]{0:T(128)} %get-tuple-element.109) | copy-start | bytes 1540
  1102.9 3.9 copy-start.23
  1102.9 3.9 copy-start.24
  1102.9 3.9 copy-start.29
  1106.9 5.6 copy-start.21
  1106.9 5.6 copy-start.22
  1106.9 5.6 copy-start.28
  1112.5 5.6 copy-start.19
  1112.5 5.6 copy-start.20
  1112.5 5.6 copy-start.27
  1126.6 53.9 %copy-start.1 = (s32[3072]{0:T(1024)S(1)}, s32[3072]{0:T(1024)}, u32[]{:S(2)}) copy-start(s32[3072]{0:T(1024)} %param.20) | copy-start | bytes 36868
Sparse Core Ops, SparseCore 0:
  193.0 124.3 all-reduce.10
  350.0 123.9 all-reduce.12
  506.5 123.9 all-reduce.14
  661.9 123.9 all-reduce.16
  818.4 123.9 all-reduce.18
  975.3 123.9 all-reduce.20
where the time goes:
time: 1190 us
  waiting for transfers between devices  793 us (67%)
  local copies, waits for them, and re-layouts  149 us (13%)
  matrix products  125 us (11%)
  blocking collectives  52.4 us (4%)
  other arithmetic  34.9 us (3%)
  starting transfers between devices  18.5 us (2%)
  between operations  14.9 us (1%)
    psum x6, waiting for transfers between devices, on_device(): prior_values = lax.psum(local_values, ('member', 'state'))  744 us
    dot_general x24, matrix products, linear_gain_fit(): jnp.dot(increment[:, lower_end:upper_end], gain_tile, preferred_element_t...  125 us
    all_to_all x1, blocking collectives, on_device(): lax.all_to_all(result, 'member', split_axis=0, concat_axis=1, tiled=True)  52.4 us
    all_to_all x1, waiting for transfers between devices, on_device(): lax.all_to_all(realization_vectors, 'member', split_axis=1, concat_axis=0...  45.9 us
  transfers between devices with their start and end apart: 11, of which 8 were waited for; matrix products, arithmetic and copies ran while one was open for 9% of the time, Pallas kernels for 0%

commit v1 on v0

--- a/solution.py
+++ b/solution.py
@@ -6,6 +6,12 @@
 BLK = 512
 NBLK = 6
 spread_eps = 1e-06
+
+
+def summed_here(x, axis):
+    terms = lax.all_gather(x, axis, axis=0, tiled=False)
+    summed = terms.sum(axis=0)
+    return summed
 
 
 def extended(shard, sides, width):
@@ -132,7 +138,7 @@
         local_values = pick_values(
             cell_values, block_rows, block_cols, first_row, tile_rows, col_count
         )
-        prior_values = lax.psum(local_values, ("member", "state"))
+        prior_values = summed_here(local_values, ("member", "state"))
         anomaly, increment, inverse = increments(
             prior_values, jnp.take(observations, chosen), jnp.take(obs_variance, chosen)
         )

time: 1190 us -> 726 us (0.61)
  waiting for transfers between devices: 793 us -> 323 us
    psum x6 -> x0, waiting for transfers between devices: 744 us -> none  [on_device(): prior_values = lax.psum(local_values, ('member', 'state'))]
    all_gather x0 -> x6, waiting for transfers between devices: none -> 292 us  [summed_here(): terms = lax.all_gather(x, axis, axis=0, tiled=False)]
    all_to_all x1, waiting for transfers between devices: 45.9 us -> 23.6 us  [on_device(): lax.all_to_all(realization_vectors, 'member', split_axis=1, concat_axis=0...]
    reduce_sum x0 -> x6, other arithmetic: none -> 15.8 us  [summed_here(): summed = terms.sum(axis=0)]
  transfers between devices with their start and end apart: 11 -> 11, of which waited for: 8 -> 9; matrix products, arithmetic and copies ran while one was open for 9% -> 14% of each run, Pallas kernels for 0% -> 0%
where the time goes in v1:
time: 726 us; the launch traced here: 717 us
  waiting for transfers between devices  323 us (44%)
  local copies, waits for them, and re-layouts  149 us (21%)
  matrix products  124 us (17%)
  blocking collectives  52 us (7%)
  other arithmetic  36.6 us (5%)
  starting transfers between devices  17.1 us (2%)
  between operations  14.7 us (2%)
    all_gather x6, waiting for transfers between devices, summed_here(): terms = lax.all_gather(x, axis, axis=0, tiled=False)  292 us
    dot_general x24, matrix products, linear_gain_fit(): jnp.dot(increment[:, lower_end:upper_end], gain_tile, preferred_element_t...  124 us
    all_to_all x1, blocking collectives, on_device(): lax.all_to_all(result, 'member', split_axis=0, concat_axis=1, tiled=True)  52 us
    all_to_all x1, waiting for transfers between devices, on_device(): lax.all_to_all(realization_vectors, 'member', split_axis=1, concat_axis=0...  23.6 us
    gather x6, local copies, waits for them, and re-layouts, on_device(): jnp.take(observations, chosen)  20 us
    gather x6, local copies, waits for them, and re-layouts, pick_values(): jnp.take(cell_values, local_index, axis=1)  19.3 us
    gather x6, local copies, waits for them, and re-layouts, on_device(): jnp.take(obs_variance, chosen)  19.2 us
    gather x6, local copies, waits for them, and re-layouts, on_device(): block_rows = jnp.take(obs_row, chosen)  18.9 us
  transfers between devices with their start and end apart: 11, of which 9 were waited for; matrix products, arithmetic and copies ran while one was open for 14% of the time, Pallas kernels for 0%

profile of v1, /device:TPU:0, one launch (start us, length us, event | category | flops | bytes accessed | tf_op | source)
XLA Modules:
  0.0 716.9 jit_solution(11982546438807816886)
XLA Ops:
  9.4 4.8 collective-permute-start.1
  16.5 3.7 collective-permute-done
  21.3 4.3 collective-permute-start.3
  27.8 3.7 collective-permute-done.2
  33.8 5.0 all-to-all-start
  64.3 23.6 %all-to-all-done = f32[8,64,1024]{2,0,1:T(8,128)S(1)} async-done(((f32[8,64,1024]{2,0,1:T(8,128)}), f32[8,64,1024]{2,0,1:T(8,128)S(1)}, u32[]{:S(2)}, u32[]{:S(2)}) %all-to-all-start) | async-done | bytes 2097184 | tf_op jit(solution)/shard_map/all_to_all | solution.py:123
  90.5 3.2 gather_fusion.2
  104.3 3.3 gather_fusion.3
  108.0 46.9 %all-gather.13.cloned.1.call-done = f32[2048,512]{1,0:T(8,128)} async-done(((f32[64,512]{1,0:T(8,128)}), f32[2048,512]{1,0:T(8,128)}) %all-gather.13.cloned.1.call-update) | async-done | bytes 4194320 | tf_op jit(solution)/shard_map/all_gather | solution.py:12
  160.1 3.9 fusion.93
  164.0 5.6 convolution_add_fusion.17
  169.6 5.6 convolution_add_fusion.16
  175.2 5.7 fusion.292
  180.8 3.8 copy.62
  188.9 3.5 gather_fusion.10
  208.3 41.3 %all-gather.15.cloned.1.call-done = f32[2048,512]{1,0:T(8,128)} async-done(((f32[64,512]{1,0:T(8,128)}), f32[2048,512]{1,0:T(8,128)}) %all-gather.15.cloned.1.call-update) | async-done | bytes 4194320 | tf_op jit(solution)/shard_map/all_gather | solution.py:12
  254.9 3.9 fusion.92
  258.8 5.6 convolution_add_fusion.14
  264.4 5.6 convolution_add_fusion.13
  270.0 5.7 fusion.295
  275.6 3.8 copy.64
  283.7 3.3 gather_fusion.16
  290.2 54.1 %all-gather.17.cloned.1.call-done = f32[2048,512]{1,0:T(8,128)} async-done(((f32[64,512]{1,0:T(8,128)}), f32[2048,512]{1,0:T(8,128)}) %all-gather.17.cloned.1.call-update) | async-done | bytes 4194320 | tf_op jit(solution)/shard_map/all_gather | solution.py:12
  349.7 3.9 fusion.91
  353.6 5.6 convolution_add_fusion.11
  359.2 5.6 convolution_add_fusion.10
  364.8 5.6 fusion.298
  377.5 3.5 gather_fusion.22
  396.9 41.3 %all-gather.19.cloned.1.call-done = f32[2048,512]{1,0:T(8,128)} async-done(((f32[64,512]{1,0:T(8,128)}), f32[2048,512]{1,0:T(8,128)}) %all-gather.19.cloned.1.call-update) | async-done | bytes 4194320 | tf_op jit(solution)/shard_map/all_gather | solution.py:12
  443.3 3.9 fusion.90
  447.2 5.6 convolution_add_fusion.8
  452.8 5.6 convolution_add_fusion.7
  458.4 5.7 fusion.301
  464.0 3.8 copy.68
  472.1 3.3 gather_fusion.28
  478.6 54.2 %all-gather.21.cloned.1.call-done = f32[2048,512]{1,0:T(8,128)} async-done(((f32[64,512]{1,0:T(8,128)}), f32[2048,512]{1,0:T(8,128)}) %all-gather.21.cloned.1.call-update) | async-done | bytes 4194320 | tf_op jit(solution)/shard_map/all_gather | solution.py:12
  538.1 3.9 fusion.89
  542.0 5.6 convolution_add_fusion.5
  547.6 5.6 convolution_add_fusion.4
  553.2 5.7 fusion.304
  558.8 3.8 copy.70
  570.0 3.4 gather_fusion.33
  573.4 54.2 %all-gather.23.cloned.1.call-done = f32[2048,512]{1,0:T(8,128)} async-done(((f32[64,512]{1,0:T(8,128)}), f32[2048,512]{1,0:T(8,128)}) %all-gather.23.cloned.1.call-update) | async-done | bytes 4194320 | tf_op jit(solution)/shard_map/all_gather | solution.py:12
  632.9 3.9 fusion.88
  636.8 5.6 convolution_add_fusion.2
  642.4 5.6 convolution_add_fusion.1
  647.9 5.6 fusion.72
  656.4 52.0 %all_to_all.33 = f32[64,8,1024]{2,1,0:T(8,128)S(1)} all-to-all(f32[64,8,1024]{2,1,0:T(8,128)S(1)} %bitcast.48), channel_id=1, replica_groups=mesh['member'=8,'state'=4] {'member'}, dimensions={0} | all-to-all | bytes 4194304 | tf_op jit(solution)/shard_map/all_to_all | solution.py:157
  (177 shorter events, 150.1 us)
Async XLA Ops:
  6.5 32.3 %copy-start = (s32[3072]{0:T(1024)S(1)}, s32[3072]{0:T(1024)}, u32[]{:S(2)}) copy-start(s32[3072]{0:T(1024)} %param.20) | copy-start | bytes 36868
  9.4 7.1 collective-permute-start.1
  14.2 6.0 copy-start.10
  14.2 5.9 collective-permute-start
  21.3 6.4 collective-permute-start.3
  25.6 5.8 collective-permute-start.2
  33.8 5.1 copy-start.11
  33.8 54.1 %all-to-all-start = ((f32[8,64,1024]{2,0,1:T(8,128)}), f32[8,64,1024]{2,0,1:T(8,128)S(1)}, u32[]{:S(2)}, u32[]{:S(2)}) async-start(f32[8,64,1024]{2,0,1:T(8,128)} %fusion.82), calls=%async_computation | async-start | bytes 4194304 | tf_op jit(solution)/shard_map/all_to_all | solution.py:123
  38.8 116.2 %all-gather.13.cloned.1.call-start = ((), (), s32[]{:S(2)}) async-start(), calls=%async_computation.2 | async-start | bytes 4325376 | tf_op jit(solution)/shard_map/all_gather | solution.py:12
  45.2 12.7 %copy-start.2 = (s32[3072]{0:T(1024)S(1)}, s32[3072]{0:T(1024)}, u32[]{:S(2)}) copy-start(s32[3072]{0:T(1024)} %param.18) | copy-start | bytes 36868
  48.4 12.7 %copy-start.3 = (s32[3072]{0:T(1024)S(1)}, s32[3072]{0:T(1024)}, u32[]{:S(2)}) copy-start(s32[3072]{0:T(1024)} %param.19) | copy-start | bytes 36868
  90.5 10.6 %copy-start.4 = (f32[3072]{0:T(1024)S(1)}, f32[3072]{0:T(1024)}, u32[]{:S(2)}) copy-start(f32[3072]{0:T(1024)} %param.16) | copy-start | bytes 36868
  90.5 13.8 %copy-start.5 = (f32[3072]{0:T(1024)S(1)}, f32[3072]{0:T(1024)}, u32[]{:S(2)}) copy-start(f32[3072]{0:T(1024)} %param.17) | copy-start | bytes 36868
  94.8 154.8 %all-gather.15.cloned.1.call-start = ((), (), s32[]{:S(2)}) async-start(), calls=%async_computation.3 | async-start | bytes 4325376 | tf_op jit(solution)/shard_map/all_gather | solution.py:12
  188.9 155.5 %all-gather.17.cloned.1.call-start = ((), (), s32[]{:S(2)}) async-start(), calls=%async_computation.4 | async-start | bytes 4325376 | tf_op jit(solution)/shard_map/all_gather | solution.py:12
  249.6 5.3 copy-start.6
  283.6 154.5 %all-gather.19.cloned.1.call-start = ((), (), s32[]{:S(2)}) async-start(), calls=%async_computation.5 | async-start | bytes 4325376 | tf_op jit(solution)/shard_map/all_gather | solution.py:12
  344.4 5.3 copy-start.8
  377.4 155.4 %all-gather.21.cloned.1.call-start = ((), (), s32[]{:S(2)}) async-start(), calls=%async_computation.6 | async-start | bytes 4325376 | tf_op jit(solution)/shard_map/all_gather | solution.py:12
  472.0 155.5 %all-gather.23.cloned.1.call-start = ((), (), s32[]{:S(2)}) async-start(), calls=%async_computation.7 | async-start | bytes 4325376 | tf_op jit(solution)/shard_map/all_gather | solution.py:12
  532.8 5.3 copy-start.7
  627.6 5.3 copy-start.9
  656.3 53.5 %copy-start.1 = (s32[3072]{0:T(1024)S(1)}, s32[3072]{0:T(1024)}, u32[]{:S(2)}) copy-start(s32[3072]{0:T(1024)} %param.20) | copy-start | bytes 36868
Sparse Core Ops, SparseCore 0:
  94.9 59.9 all-gather.12
  189.0 60.5 all-gather.14
  283.8 60.5 all-gather.16
  377.5 60.5 all-gather.18
  472.2 60.5 all-gather.20
  566.9 60.5 all-gather.22
